TPU v7x, 256 devices: a whole 4x4x8 slice. The times are simulated.
256 devices in a mesh: ctx: 32 (over z, y), head: 8 (over x, core).
Axes of the slice: x: 4, y: 4, z: 8, core: 2. Of those that a mesh axis runs over, the one named last changes fastest.
Arguments:
- queries: bfloat16 [32768, 4096], P('ctx', 'head'), may hold values from -110 to 110
- keys: bfloat16 [32768, 1024], P('ctx', 'head'), may hold values from -4 to 4
- values: bfloat16 [32768, 1024], P('ctx', 'head'), may hold values from -6 to 6
- pairs: int32 [256, 8], P('ctx'), may hold values from -1 to 255, as said below
- positions: int32 [1024], replicated, may hold values from 0 to 32767, as said below
- w_out: bfloat16 [4096, 4096], P('head', 'ctx'), may hold values from -0.09375 to 0.09375
Outputs:
- mixed: bfloat16 [32768, 4096], P(('ctx', 'head'))
Inputs may be any that keep to these rules, and one draw needn't show every extreme that they name: `pairs`: entry l of query block b is either b XOR 2^l or -1, and is -1 whenever 2^l >= 256. `positions`: distinct and ascending; exactly 32 of them lie in each index of ctx's 1024 tokens.
All inputs are finite; a program needn't handle non-finite values.
Results may differ from a plain program's by a relative error of at most 0.0057.
Values may be sent and summed in bfloat16 or wider, within the bound.
A program may use at most 64 MiB of HBM per device.

v0:
```python
import math

import jax
import jax.numpy as jnp
from jax import lax
from jax.sharding import PartitionSpec as P

HD = 128
BLK = 128


def swapped(value, axis, bit):
    return lax.ppermute(value, axis, [(i, i ^ 1 << bit) for i in range(lax.axis_size(axis))])


def shards(queries, keys, values, pairs, positions, w_out):
    tokens_here = keys.shape[0]
    kv_here = keys.shape[1] // HD
    groups = queries.shape[1] // keys.shape[1]
    blocks_here = tokens_here // BLK
    local_bits = blocks_here.bit_length() - 1
    ctx_bits = lax.axis_size("ctx").bit_length() - 1
    width = 2 * kv_here * HD
    joined = jnp.concatenate([keys, values], axis=1)
    tiles = joined.reshape(blocks_here, BLK, width)
    partner_tiles = []
    for level in range(local_bits):
        span = 1 << level
        paired = tiles.reshape(blocks_here // (2 * span), 2, span, BLK, width)
        partner_tiles.append(jnp.flip(paired, axis=1).reshape(blocks_here, BLK, width))
    for bit in range(ctx_bits):
        partner_tiles.append(swapped(tiles, "ctx", bit))
    used = local_bits + ctx_bits
    start = lax.axis_index("ctx") * tokens_here
    columns = jnp.arange(tokens_here, dtype=jnp.int32)
    selector = (positions[:, None] - start == columns[None, :]).astype(jnp.bfloat16)
    picked = jnp.dot(selector, joined, preferred_element_type=jnp.float32)
    global_rows = lax.psum(picked.astype(jnp.bfloat16), "ctx")
    partner_stack = jnp.stack(partner_tiles, axis=1)
    flags = pairs >= 0
    query_tiles = queries.reshape(blocks_here, BLK, kv_here, groups, HD)
    scale = 1.0 / math.sqrt(HD)
    global_count = global_rows.shape[0]

    def attend(items):
        query_tile, own_tile, partner_tile, flag_row = items
        key_set = jnp.concatenate(
            [own_tile, partner_tile.reshape(used * BLK, width), global_rows], axis=0
        )
        key_count = key_set.shape[0]
        key_part = key_set[:, : kv_here * HD].reshape(key_count, kv_here, HD)
        value_part = key_set[:, kv_here * HD :].reshape(key_count, kv_here, HD)
        visible = jnp.concatenate(
            [
                jnp.ones((BLK,), jnp.bool_),
                jnp.repeat(flag_row, BLK),
                jnp.ones((global_count,), jnp.bool_),
            ]
        )
        scores = (
            jnp.einsum("qkgd,nkd->qkgn", query_tile, key_part, preferred_element_type=jnp.float32)
            * scale
        )
        scores = jnp.where(visible, scores, -jnp.inf)
        top = jnp.max(scores, axis=-1, keepdims=True)
        weights = jnp.exp(scores - top)
        total = jnp.sum(weights, axis=-1, keepdims=True)
        rounded = weights.astype(jnp.bfloat16)
        result = (
            jnp.einsum("qkgn,nkd->qkgd", rounded, value_part, preferred_element_type=jnp.float32)
            / total
        )
        return result.astype(jnp.bfloat16).reshape(BLK, kv_here * groups * HD)

    attended = lax.map(attend, (query_tiles, tiles, partner_stack, flags)).reshape(
        tokens_here, kv_here * groups * HD
    )
    w_full = lax.all_gather(w_out, "ctx", axis=1, tiled=True)
    return lax.psum_scatter(
        jnp.dot(attended, w_full, preferred_element_type=jnp.float32),
        "head",
        scatter_dimension=0,
        tiled=True,
    ).astype(jnp.bfloat16)


def solution(mesh):
    return jax.shard_map(
        shards,
        mesh=mesh,
        in_specs=(
            P("ctx", "head"),
            P("ctx", "head"),
            P("ctx", "head"),
            P("ctx", None),
            P(),
            P("head", "ctx"),
        ),
        out_specs=P(("ctx", "head"), None),
        check_vma=False,
    )
```

profile of v0, /device:TPU:1, one launch (start us, length us, event | category | flops | bytes accessed | tf_op | source)
XLA Modules:
  0.0 384.6 jit_solution(14389581057795682204)
XLA Ops:
  6.5 1.0 constant_dynamic-update-slice_fusion.2
  8.2 1.0 constant_dynamic-update-slice_fusion.1
  9.3 1.6 fusion.20
  11.0 7.8 %collective-permute-start.4 = (bf16[8,128,256]{2,1,0:T(8,128)(2,1)S(1)}, bf16[8,128,256]{2,1,0:T(8,128)(2,1)S(1)}, u32[]{:S(2)}, u32[]{:S(2)}) collective-permute-start(bf16[8,128,256]{2,1,0:T(8,128)(2,1)S(1)} %bitcast.89), channel_id=1, source_target_pairs={{0,128},{8,136},{16,144},{24,152},{32,160},{40,168},{48,176},{56,1... | collective-permute-start | bytes 1572872 | tf_op jit(solution)/shard_map/ppermute | solution.py:13
  18.8 1.2 collective-permute-start.3
  20.7 2.9 collective-permute-start.1
  24.2 0.8 constant_dynamic-update-slice_fusion.5
  25.1 0.9 constant_dynamic-update-slice_fusion.4
  26.0 0.9 constant_dynamic-update-slice_fusion.3
  27.1 19.7 %collective-permute-done = bf16[8,128,256]{2,1,0:T(8,128)(2,1)} collective-permute-done((bf16[8,128,256]{2,1,0:T(8,128)(2,1)S(1)}, bf16[8,128,256]{2,1,0:T(8,128)(2,1)}, u32[]{:S(2)}, u32[]{:S(2)}) %collective-permute-start) | collective-permute-done | bytes 524320 | tf_op jit(solution)/shard_map/ppermute | solution.py:13
  46.9 1.9 bitcast_dynamic-update-slice_fusion.4
  48.8 1.9 bitcast_dynamic-update-slice_fusion.3
  50.7 13.8 %collective-permute-done.2 = bf16[8,128,256]{2,1,0:T(8,128)(2,1)} collective-permute-done((bf16[8,128,256]{2,1,0:T(8,128)(2,1)S(1)}, bf16[8,128,256]{2,1,0:T(8,128)(2,1)}, u32[]{:S(2)}, u32[]{:S(2)}) %collective-permute-start.2) | collective-permute-done | bytes 524320 | tf_op jit(solution)/shard_map/ppermute | solution.py:13
  64.5 1.9 bitcast_dynamic-update-slice_fusion.2
  66.4 2.2 collective-permute-done.3
  68.6 1.9 bitcast_dynamic-update-slice_fusion.1
  70.5 0.9 bitcast_dynamic-update-slice_fusion
  71.3 109.7 %all-reduce.2.cloned.1.call-done = bf16[1024,256]{1,0:T(8,128)(2,1)} async-done(((bf16[1024,256]{1,0:T(8,128)(2,1)}), bf16[1024,256]{1,0:T(8,128)(2,1)}) %all-reduce.2.cloned.1.call-update) | async-done | bytes 524304 | tf_op jit(solution)/shard_map/psum | solution.py:38
  181.1 43.7 %while.10 = (s32[]{:T(128)}, bf16[8,128,512]{2,1,0:T(8,128)(2,1)}, bf16[8,128,256]{2,1,0:T(8,128)(2,1)S(1)}, bf16[8,8,128,256]{3,2,1,0:T(8,128)(2,1)}, bf16[1024...) while((s32[]{:T(128)}, bf16[8,128,512]{2,1,0:T(8,128)(2,1)}, ...), condition=%wide.region_4.5_spmd, body=%wide.region_1.4_spmd.sunk | while | flops 581700864 | bytes 18959892 | solution.py:75
  181.3 1.1 constant_dynamic-slice_fusion.5
  182.4 1.1 pad_maximum_fusion.2
  184.9 0.9 fusion.33
  186.7 1.1 constant_dynamic-slice_fusion.5
  187.8 1.1 pad_maximum_fusion.2
  188.9 0.8 fusion.31
  190.3 0.9 fusion.33
  192.2 1.1 constant_dynamic-slice_fusion.5
  193.3 1.1 pad_maximum_fusion.2
  195.8 0.9 fusion.33
  197.7 1.1 constant_dynamic-slice_fusion.5
  198.8 1.1 pad_maximum_fusion.2
  201.3 0.9 fusion.33
  203.1 1.1 constant_dynamic-slice_fusion.5
  204.2 1.1 pad_maximum_fusion.2
  206.7 0.9 fusion.33
  208.6 1.1 constant_dynamic-slice_fusion.5
  209.7 1.1 pad_maximum_fusion.2
  212.2 0.9 fusion.33
  214.1 1.1 constant_dynamic-slice_fusion.5
  215.2 1.1 pad_maximum_fusion.2
  217.7 0.9 fusion.33
  219.6 1.1 constant_dynamic-slice_fusion.5
  220.6 1.1 pad_maximum_fusion.2
  223.1 0.9 fusion.33
  224.8 40.6 %all-gather.2.cloned.1.call-done = bf16[512,4096]{1,0:T(8,128)(2,1)} async-done(((bf16[512,128]{1,0:T(8,128)(2,1)}), bf16[512,4096]{1,0:T(8,128)(2,1)}) %all-gather.2.cloned.1.call-update) | async-done | bytes 4194320 | tf_op jit(solution)/shard_map/all_gather | solution.py:78
  265.4 12.8 %fusion.22 = f32[1024,4096]{1,0:T(8,128)} fusion(bf16[1024,512]{1,0:T(8,128)(2,1)} %bitcast.101, bf16[512,4096]{1,0:T(8,128)(2,1)} %all-gather.2.cloned.1.call-done), kind=kOutput, calls=%fused_computation.41 | convolution fusion | flops 4294967296 | bytes 22020096 | tf_op jit(solution)/shard_map/dot_general | solution.py:80
  278.2 97.2 %reduce-scatter.2.cloned.1.call-done = f32[128,4096]{1,0:T(8,128)} async-done(((f32[1024,4096]{1,0:T(8,128)}), f32[128,4096]{1,0:T(8,128)}) %reduce-scatter.2.cloned.1.call-update) | async-done | bytes 2097168 | tf_op jit(solution)/shard_map/reduce_scatter | solution.py:79
  375.4 2.7 convert_element_type.17
  (108 shorter events, 20.2 us)
Async XLA Ops:
  6.5 17.6 %copy-start.1 = (s32[8,8]{1,0:T(8,128)S(1)}, s32[8,8]{1,0:T(8,128)}, u32[]{:S(2)}) copy-start(s32[8,8]{1,0:T(8,128)} %param.11) | copy-start | bytes 772
  6.5 174.5 %all-reduce.2.cloned.1.call-start = ((), (), s32[]{:S(2)}) async-start(), calls=%async_computation.1 | async-start | bytes 1048576 | tf_op jit(solution)/shard_map/psum | solution.py:38
  10.9 16.0 %copy-start = (bf16[1024,512]{1,0:T(8,128)(2,1)S(1)}, bf16[1024,512]{1,0:T(8,128)(2,1)}, u32[]{:S(2)}) copy-start(bf16[1024,512]{1,0:T(8,128)(2,1)} %param.8) | copy-start | bytes 3145732
  10.9 254.5 %all-gather.2.cloned.1.call-start = ((), (), s32[]{:S(2)}) async-start(), calls=%async_computation.2 | async-start | bytes 4325376 | tf_op jit(solution)/shard_map/all_gather | solution.py:78
  11.0 59.5 %collective-permute-start.4 = (bf16[8,128,256]{2,1,0:T(8,128)(2,1)S(1)}, bf16[8,128,256]{2,1,0:T(8,128)(2,1)S(1)}, u32[]{:S(2)}, u32[]{:S(2)}) collective-permute-start(bf16[8,128,256]{2,1,0:T(8,128)(2,1)S(1)} %bitcast.89), channel_id=1, source_target_pairs={{0,128},{8,136},{16,144},{24,152},{32,160},{40,168},{48,176},{56,1... | collective-permute-start | bytes 1572872 | tf_op jit(solution)/shard_map/ppermute | solution.py:13
  18.8 49.8 %collective-permute-start.3 = (bf16[8,128,256]{2,1,0:T(8,128)(2,1)S(1)}, bf16[8,128,256]{2,1,0:T(8,128)(2,1)}, u32[]{:S(2)}, u32[]{:S(2)}) collective-permute-start(bf16[8,128,256]{2,1,0:T(8,128)(2,1)S(1)} %bitcast.90), channel_id=1, source_target_pairs={{0,64},{8,72},{16,80},{24,88},{32,96},{40,104},{48,112},{56,120},{... | collective-permute-start | bytes 1572872 | tf_op jit(solution)/shard_map/ppermute | solution.py:13
  20.0 44.5 %collective-permute-start.2 = (bf16[8,128,256]{2,1,0:T(8,128)(2,1)S(1)}, bf16[8,128,256]{2,1,0:T(8,128)(2,1)}, u32[]{:S(2)}, u32[]{:S(2)}) collective-permute-start(bf16[8,128,256]{2,1,0:T(8,128)(2,1)S(1)} %bitcast.91), channel_id=1, source_target_pairs={{0,32},{8,40},{16,48},{24,56},{32,0},{40,8},{48,16},{56,24},{64,96... | collective-permute-start | bytes 1572872 | tf_op jit(solution)/shard_map/ppermute | solution.py:13
  20.7 28.1 %collective-permute-start.1 = (bf16[8,128,256]{2,1,0:T(8,128)(2,1)S(1)}, bf16[8,128,256]{2,1,0:T(8,128)(2,1)}, u32[]{:S(2)}, u32[]{:S(2)}) collective-permute-start(bf16[8,128,256]{2,1,0:T(8,128)(2,1)S(1)} %bitcast.92), channel_id=1, source_target_pairs={{0,16},{8,24},{16,0},{24,8},{32,48},{40,56},{48,32},{56,40},{64,80... | collective-permute-start | bytes 1572872 | tf_op jit(solution)/shard_map/ppermute | solution.py:13
  23.6 23.2 %collective-permute-start = (bf16[8,128,256]{2,1,0:T(8,128)(2,1)S(1)}, bf16[8,128,256]{2,1,0:T(8,128)(2,1)}, u32[]{:S(2)}, u32[]{:S(2)}) collective-permute-start(bf16[8,128,256]{2,1,0:T(8,128)(2,1)S(1)} %bitcast.93), channel_id=1, source_target_pairs={{0,8},{8,0},{16,24},{24,16},{32,40},{40,32},{48,56},{56,48},{64,72... | collective-permute-start | bytes 1572872 | tf_op jit(solution)/shard_map/ppermute | solution.py:13
  24.1 351.3 %reduce-scatter.2.cloned.1.call-start = ((), (), s32[]{:S(2)}) async-start(), calls=%async_computation.3 | async-start | bytes 18874368 | tf_op jit(solution)/shard_map/reduce_scatter | solution.py:79
Sparse Core Ops, SparseCore 0:
  11.0 169.9 all-reduce.1
  183.8 81.4 all-gather.1
  278.3 97.0 reduce-scatter.1
where the time goes:
time: 386 us; the launch traced here: 385 us
  waiting for transfers between devices  283 us (73%)
  local copies, waits for them, and re-layouts  29.7 us (8%)
  matrix products  27.7 us (7%)
  other arithmetic  17.2 us (4%)
  between operations  13.2 us (3%)
  starting transfers between devices  13.1 us (3%)
    psum x1, waiting for transfers between devices, shards(): global_rows = lax.psum(picked.astype(jnp.bfloat16), 'ctx')  110 us
    reduce_scatter x1, waiting for transfers between devices, shards(): lax.psum_scatter(jnp.dot(attended, w_full, preferred_element_type=jnp.flo...  97.2 us
    all_gather x1, waiting for transfers between devices, shards(): w_full = lax.all_gather(w_out, 'ctx', axis=1, tiled=True)  40.6 us
    ppermute x5, waiting for transfers between devices, swapped(): lax.ppermute(value, axis, [(i, i ^ 1 << bit) for i in range(lax.axis_size...  35.7 us
    ppermute x5, starting transfers between devices, swapped(): lax.ppermute(value, axis, [(i, i ^ 1 << bit) for i in range(lax.axis_size...  13.1 us
    dot_general x1, matrix products, shards(): jnp.dot(attended, w_full, preferred_element_type=jnp.float32)  12.8 us
    unnamed x12, local copies, waits for them, and re-layouts  11.2 us
    dynamic_slice x16, local copies, waits for them, and re-layouts, shards(): lax.map(attend, (query_tiles, tiles, partner_stack, flags))  9.13 us
  transfers between devices with their start and end apart: 8, of which 6 were waited for; matrix products, arithmetic and copies ran while one was open for 14% of the time, Pallas kernels for 0%

commit v1 on v0

v1 whole, which is shorter than its diff:
```python
import math

import jax
import jax.numpy as jnp
from jax import lax
from jax.experimental import pallas as pl
from jax.experimental.pallas import tpu as pltpu
from jax.sharding import PartitionSpec as P

HD = 128
BLK = 128
BLOCKS = 8
CHUNKS = 4
ROWS = 2 * BLK
GROUPS = 4
NY, NZ, NX = 4, 8, 4
PICK = 32
KEYS = 9 * BLK + NY * NZ * PICK
SCALE = math.log2(math.e) / math.sqrt(HD)
MESH = pl.DeviceIdType.MESH
ORDER = (2, 1, 3, 0)


def flip(value, span):
    return value + span - 2 * span * ((value // span) % 2)


def kernel(
    q_hbm, k_hbm, v_hbm, pairs_ref, pos_ref, w_hbm, out_ref,
    q_ref, kv_own, kv_in, g_ref, w_own, w_sib, s_ref, p_ref, att_ref, att_in,
    p_send, r1a, r1b, r2a, r2b, acc_ref,
    load_sem, kv_ssem, kv_rsem, g_ssem, g_rsem, zu_s, zu_r, zd_s, zd_r,
    yu_s, yu_r, yd_s, yd_r, far_s, far_r, sib_s, sib_r, att_s, att_r,
    one_s, one_r, two_s, two_r,
):
    ctx = lax.axis_index("ctx")
    head = lax.axis_index("head")
    z, y = ctx // NY, ctx % NY
    x, core = head // 2, head % 2

    def at(zz, yy):
        return (zz * NY + yy, head)

    z_up, z_dn = (z + 1) % NZ, (z + NZ - 1) % NZ
    y_up, y_dn, y_far = (y + 1) % NY, (y + NY - 1) % NY, (y + 2) % NY
    zu, zd, yu, yd, yf = at(z_up, y), at(z_dn, y), at(z, y_up), at(z, y_dn), at(z, y_far)
    sibling = (ctx, flip(head, 1))
    xu = (ctx, ((x + 1) % NX) * 2 + core)
    xd = (ctx, ((x + NX - 1) % NX) * 2 + core)
    partners = (at(z, flip(y, 1)), yf, at(flip(z, 1), y), at(flip(z, 2), y), at((z + 4) % NZ, y))

    loads = [
        pltpu.make_async_copy(w_hbm, w_own.at[y, z], load_sem.at[0]),
        pltpu.make_async_copy(k_hbm, kv_own.at[:, 0], load_sem.at[1]),
        pltpu.make_async_copy(v_hbm, kv_own.at[:, 1], load_sem.at[2]),
        pltpu.make_async_copy(q_hbm, q_ref, load_sem.at[3]),
    ]
    for load in loads:
        load.start()

    barrier = pltpu.get_barrier_semaphore()
    peers = (zu, zd, yu, yd, yf, partners[3], partners[4], sibling, xu, xd)
    for peer in peers:
        pl.semaphore_signal(barrier, inc=1, device_id=peer, device_id_type=MESH)
    pl.semaphore_wait(barrier, len(peers))

    sent = []

    def send(src, dst, ssem, rsem, device):
        copy = pltpu.make_async_remote_copy(
            src_ref=src, dst_ref=dst, send_sem=ssem, recv_sem=rsem,
            device_id=device, device_id_type=MESH,
        )
        copy.start()
        sent.append(copy)

    def arrived(dst, rsem):
        pltpu.make_async_copy(dst, dst, rsem).wait()

    slots = [z, z_dn, z_up, (z + 6) % NZ, (z + 2) % NZ, (z + 5) % NZ, (z + 3) % NZ, (z + 4) % NZ]

    def spread(e):
        ref = w_own.at[y, slots[e]]
        send(ref, ref, yu_s.at[e], yu_r.at[e], yu)
        send(ref, ref, yd_s.at[e], yd_r.at[e], yd)

    def z_step(t):
        if t > 0:
            arrived(w_own.at[y, slots[2 * t - 1]], zu_r.at[t - 1])
        if t < 4:
            ref = w_own.at[y, z if t == 0 else slots[2 * t - 1]]
            send(ref, ref, zu_s.at[t], zu_r.at[t], zu)
        if 0 < t < 4:
            arrived(w_own.at[y, slots[2 * t]], zd_r.at[t - 1])
        if t < 3:
            ref = w_own.at[y, slots[2 * t]]
            send(ref, ref, zd_s.at[t], zd_r.at[t], zd)
        if t == 0:
            spread(0)
        else:
            spread(2 * t - 1)
            if t < 4:
                spread(2 * t)

    def y_step(e):
        low, high = w_own.at[y_dn, slots[e]], w_own.at[y_up, slots[e]]
        arrived(low, yu_r.at[e])
        if e % 2 == 0:
            send(low, low, far_s.at[e], far_r.at[e], yu)
        arrived(high, yd_r.at[e])
        if e % 2 == 1:
            send(high, high, far_s.at[e], far_r.at[e], yd)

    def share(n, yy):
        send(w_own.at[yy], w_sib.at[yy], sib_s.at[n], sib_r.at[n], sibling)

    def kv_send(s):
        i = (x + ORDER[s]) % NX
        for n in (4, 3, 2, 1, 0):
            send(kv_own.at[i], kv_in.at[n, i], kv_ssem.at[n, s], kv_rsem.at[n, s], partners[n])

    loads[0].wait()
    z_step(0)
    loads[1].wait()
    loads[2].wait()
    kv_send(0)

    wanted = pos_ref[pl.ds(ctx, 1), :]
    zpos = z // 4 + 2 * ((z // 2) % 2) + 4 * (z % 2)
    for part in range(2):
        picked = jnp.zeros((PICK, HD), jnp.float32)
        for i in range(CHUNKS):
            spot = lax.broadcasted_iota(jnp.int32, (ROWS, PICK), 0) + (ctx * 1024 + i * ROWS)
            chosen = (spot == wanted).astype(jnp.float32).astype(jnp.bfloat16)
            picked += lax.dot_general(
                chosen, kv_own[i, part], (((0,), (0,)), ((), ())),
                preferred_element_type=jnp.float32,
            )
        g_ref[part, y, pl.ds(pl.multiple_of(zpos * PICK, PICK), PICK), :] = picked.astype(jnp.bfloat16)

    def g_rows(yy, size, slot):
        start = (slot // size) * size * PICK
        return g_ref.at[:, yy, pl.ds(pl.multiple_of(start, size * PICK), size * PICK), :]

    for n, partner in enumerate((partners[4], partners[3], partners[2])):
        size = 1 << n
        mine = g_rows(y, size, zpos)
        send(mine, mine, g_ssem.at[n], g_rsem.at[n], partner)
        arrived(g_rows(y, size, flip(zpos, size)), g_rsem.at[n])
        if n < 2:
            z_step(n + 1)
    whole = g_ref.at[:, y]
    for n, peer in enumerate((yu, yd, yf)):
        send(whole, whole, g_ssem.at[3 + n], g_rsem.at[3 + n], peer)
    kv_send(1)
    z_step(3)
    for n, yy in enumerate((y_dn, y_up, y_far)):
        arrived(g_ref.at[:, yy], g_rsem.at[3 + n])
    loads[3].wait()

    def attend(i, t):
        j = 2 * i + t
        own = [j, flip(j, 1), flip(j, 2), flip(j, 4)]

        def block(part, n):
            if n < 4:
                jj = own[n]
                return kv_own[jj // 2, part, pl.ds(pl.multiple_of((jj % 2) * BLK, BLK), BLK), :]
            return kv_in[n - 4, i, part, pl.ds(t * BLK, BLK), :]

        rows = pl.ds(pl.multiple_of(j * BLK, BLK), BLK)
        queries = jnp.concatenate(
            [q_ref[rows, h * HD : (h + 1) * HD] for h in range(GROUPS)], axis=0
        )
        contract = (((1,), (1,)), ((), ()))

        def bias(n):
            return jnp.where(pairs_ref[j, n - 1] >= 0, 0.0, -jnp.inf).astype(jnp.float32)

        for first in range(0, 9, 2):
            names = list(range(first, min(first + 2, 9)))
            keys = jnp.concatenate([block(0, n) for n in names], axis=0)
            scores = lax.dot_general(queries, keys, contract, preferred_element_type=jnp.float32)
            for m, n in enumerate(names):
                part = scores[:, m * BLK : (m + 1) * BLK]
                if n > 0:
                    part = part + bias(n)
                s_ref[:, n * BLK : (n + 1) * BLK] = part
        for yy in range(NY):
            start = 9 * BLK + yy * NZ * PICK
            s_ref[:, start : start + NZ * PICK] = lax.dot_general(
                queries, g_ref[0, yy], contract, preferred_element_type=jnp.float32
            )
        totals = []
        for r in range(0, GROUPS * BLK, 64):
            scores = s_ref[r : r + 64, :]
            top = jnp.max(scores, axis=1, keepdims=True)
            weights = jnp.exp2((scores - top) * SCALE)
            totals.append(jnp.sum(weights, axis=1, keepdims=True))
            p_ref[r : r + 64, :] = weights.astype(jnp.bfloat16)
        values = jnp.concatenate(
            [block(1, n) for n in range(9)] + [g_ref[1, yy] for yy in range(NY)], axis=0
        )
        result = jnp.dot(p_ref[...], values, preferred_element_type=jnp.float32)
        result = (result / jnp.concatenate(totals, axis=0)).astype(jnp.bfloat16)
        for h in range(GROUPS):
            att_ref[i, t, :, h * HD : (h + 1) * HD] = result[h * BLK : (h + 1) * BLK]

    for s in range(CHUNKS):
        i = (x + ORDER[s]) % NX
        for n in range(5):
            arrived(kv_in.at[n, i], kv_rsem.at[n, s])
        for t in range(2):
            attend(i, t)
        send(att_ref.at[i, 1 - core], att_in.at[i], att_s.at[s], att_r.at[s], sibling)
        if s == 0:
            kv_send(2)
            z_step(4)
            share(0, y)
            for e in range(4):
                y_step(e)
        if s == 1:
            kv_send(3)
            for e in range(4, 8):
                y_step(e)
            share(1, y_dn)
            share(2, y_up)
        if s == 2:
            for e in range(8):
                arrived(w_own.at[y_far, slots[e]], far_r.at[e])
            share(3, y_far)

    for n, yy in enumerate((y, y_up, y_dn, y_far)):
        arrived(w_sib.at[yy], sib_r.at[(0, 2, 1, 3)[n]])

    def project(i, q, extra, put):
        left, right = att_ref[i, core], att_in[i]
        for half in range(4):
            zz, yy = 2 * q + half // 2, 2 * (half % 2)
            columns = slice(half * 256, half * 256 + 256)
            total = jnp.dot(
                left, jnp.concatenate([w_own[yy, zz], w_own[yy + 1, zz]], axis=1),
                preferred_element_type=jnp.float32,
            ) + jnp.dot(
                right, jnp.concatenate([w_sib[yy, zz], w_sib[yy + 1, zz]], axis=1),
                preferred_element_type=jnp.float32,
            )
            if extra is not None:
                total = total + extra[:, columns].astype(jnp.float32)
            put(columns, total)

    def project_send(n, i, q, extra, dst, ssem, rsem, device):
        def put(columns, total):
            p_send[n, q, :, columns] = total.astype(jnp.bfloat16)

        project(i, q, extra, put)
        send(p_send.at[n, q], dst, ssem, rsem, device)

    for s in range(CHUNKS):
        i = (x + ORDER[s]) % NX
        arrived(att_in.at[i], att_r.at[s])
    far, up, down = (x + 2) % NX, (x + 1) % NX, (x + 3) % NX
    for q in (0, 2, 1, 3):
        dst, device = (r1a.at[q], xu) if q < 2 else (r1b.at[q - 2], xd)
        project_send(0, far, q, None, dst, one_s.at[q], one_r.at[q], device)
    for q in (2, 3):
        project_send(1, up, q, None, r2a.at[q], two_s.at[q], two_r.at[q], xu)
        project_send(2, down, q - 2, None, r2b.at[q - 2], two_s.at[q + 2], two_r.at[q + 2], xd)
    for q in (0, 1):
        arrived(r1a.at[q], one_r.at[q])
        project_send(1, up, q, r1a.at[q], r2a.at[q], two_s.at[q], two_r.at[q], xu)
        arrived(r1b.at[q], one_r.at[q + 2])
        project_send(2, down, q + 2, r1b.at[q], r2b.at[q + 2], two_s.at[q + 6], two_r.at[q + 6], xd)

    for q in range(4):

        def put(columns, total, q=q):
            acc_ref[q, :, columns] = total

        project(x, q, None, put)
    for q in (2, 0, 3, 1):
        arrived(r2a.at[q], two_r.at[q])
        arrived(r2b.at[q], two_r.at[q + 4])
        out_ref[:, q * 1024 : q * 1024 + 1024] = (
            acc_ref[q] + r2a[q].astype(jnp.float32) + r2b[q].astype(jnp.float32)
        ).astype(jnp.bfloat16)
    for copy in sent:
        copy.wait_send()


def shards(queries, keys, values, pairs, positions, w_out):
    bf16, f32 = jnp.bfloat16, jnp.float32
    dma = pltpu.SemaphoreType.DMA
    hbm = pl.BlockSpec(memory_space=pl.ANY)
    return pl.pallas_call(
        kernel,
        out_shape=jax.ShapeDtypeStruct((BLK, 4096), bf16),
        in_specs=[
            hbm, hbm, hbm,
            pl.BlockSpec(memory_space=pltpu.SMEM),
            pl.BlockSpec(memory_space=pltpu.VMEM),
            hbm,
        ],
        out_specs=pl.BlockSpec(memory_space=pltpu.VMEM),
        scratch_shapes=[
            pltpu.VMEM((1024, GROUPS * HD), bf16),
            pltpu.VMEM((CHUNKS, 2, ROWS, HD), bf16),
            pltpu.VMEM((5, CHUNKS, 2, ROWS, HD), bf16),
            pltpu.VMEM((2, NY, NZ * PICK, HD), bf16),
            pltpu.VMEM((NY, NZ, 512, HD), bf16),
            pltpu.VMEM((NY, NZ, 512, HD), bf16),
            pltpu.VMEM((GROUPS * BLK, KEYS), f32),
            pltpu.VMEM((GROUPS * BLK, KEYS), bf16),
            pltpu.VMEM((CHUNKS, 2, BLK, GROUPS * HD), bf16),
            pltpu.VMEM((CHUNKS, BLK, GROUPS * HD), bf16),
            pltpu.VMEM((3, 4, BLK, 1024), bf16),
            pltpu.VMEM((2, BLK, 1024), bf16),
            pltpu.VMEM((2, BLK, 1024), bf16),
            pltpu.VMEM((4, BLK, 1024), bf16),
            pltpu.VMEM((4, BLK, 1024), bf16),
            pltpu.VMEM((4, BLK, 1024), f32),
            dma((4,)), dma((5, CHUNKS)), dma((5, CHUNKS)), dma((6,)), dma((6,)),
            dma((4,)), dma((4,)), dma((3,)), dma((3,)),
            dma((8,)), dma((8,)), dma((8,)), dma((8,)), dma((8,)), dma((8,)),
            dma((4,)), dma((4,)), dma((4,)), dma((4,)),
            dma((4,)), dma((4,)), dma((8,)), dma((8,)),
        ],
        compiler_params=pltpu.CompilerParams(
            collective_id=0, has_side_effects=True, vmem_limit_bytes=56 * 2**20
        ),
        name="butterfly",
    )(
        queries,
        keys.reshape(CHUNKS, ROWS, HD),
        values.reshape(CHUNKS, ROWS, HD),
        pairs,
        positions.reshape(NY * NZ, PICK),
        w_out,
    )


def solution(mesh):
    return jax.shard_map(
        shards,
        mesh=mesh,
        in_specs=(
            P("ctx", "head"),
            P("ctx", "head"),
            P("ctx", "head"),
            P("ctx", None),
            P(),
            P("head", "ctx"),
        ),
        out_specs=P(("ctx", "head"), None),
        check_vma=False,
    )
```

time: 386 us -> 130 us (0.34)
  waiting for transfers between devices: 283 us -> 0 us
  Pallas kernels: 0 us -> 126 us
  matrix products: 27.7 us -> 0 us
  local copies, waits for them, and re-layouts: 29.7 us -> 3.65 us
  other arithmetic: 17.2 us -> 0 us
  between operations: 13.2 us -> 0.01 us
  starting transfers between devices: 13.1 us -> 0 us
    pallas_call x0 -> x1, Pallas kernels: none -> 126 us  [shards(): pl.pallas_call(kernel, out_shape=jax.ShapeDtypeStruct((BLK, 4096), bf16),...]
    psum x1 -> x0, waiting for transfers between devices: 110 us -> none  [shards(): global_rows = lax.psum(picked.astype(jnp.bfloat16), 'ctx')]
    reduce_scatter x1 -> x0, waiting for transfers between devices: 97.2 us -> none  [shards(): lax.psum_scatter(jnp.dot(attended, w_full, preferred_element_type=jnp.flo...]
    all_gather x1 -> x0, waiting for transfers between devices: 40.6 us -> none  [shards(): w_full = lax.all_gather(w_out, 'ctx', axis=1, tiled=True)]
    ppermute x5 -> x0, waiting for transfers between devices: 35.7 us -> none  [swapped(): lax.ppermute(value, axis, [(i, i ^ 1 << bit) for i in range(lax.axis_size...]
    dot_general x18 -> x0, matrix products: 27.7 us -> none  [the longest x1 12.8 us: shards(): jnp.dot(attended, w_full, preferred_element_type=jnp.float32)]
    ppermute x5 -> x0, starting transfers between devices: 13.1 us -> none  [swapped(): lax.ppermute(value, axis, [(i, i ^ 1 << bit) for i in range(lax.axis_size...]
    dynamic_slice x16 -> x0, local copies, waits for them, and re-layouts: 9.13 us -> none  [shards(): lax.map(attend, (query_tiles, tiles, partner_stack, flags))]
  transfers between devices with their start and end apart: 8 -> 0, of which waited for: 6 -> 0; matrix products, arithmetic and copies ran while one was open for 14% -> 0% of each run, Pallas kernels for 0% -> 0%
where the time goes in v1:
time: 130 us
  Pallas kernels  126 us (97%)
  local copies, waits for them, and re-layouts  3.65 us (3%)
    pallas_call x1, Pallas kernels, shards(): pl.pallas_call(kernel, out_shape=jax.ShapeDtypeStruct((BLK, 4096), bf16),...  126 us

profile of v1, /device:TPU:1, one launch (start us, length us, event | category | flops | bytes accessed | tf_op | source)
XLA Modules:
  0.0 129.7 jit_solution(11444163219855862362)
XLA Ops:
  0.0 1.4 %reshape.11.pos_ref = s32[32,32]{1,0:T(8,128)} reshape(s32[1024]{0:T(1024)} %param.10) | data formatting | bytes 8192 | tf_op jit(solution)/shard_map/reshape | solution.py:337
  1.4 126.0 %butterfly.1 = bf16[128,4096]{1,0:T(8,128)(2,1)} custom-call(bf16[1024,512]{1,0:T(8,128)(2,1)} %q_hbm.1, bf16[4,256,128]{2,1,0:T(8,128)(2,1)} %bitcast.2, bf16[4,256,128]{2,1,0:T(8,128)(2,1)} %bitcast.3, s32[8,8]{1,0:T(8,128)} %pairs_ref.1, s32[32,32]{1,0:T(8,128)} %reshape.11.pos_ref, bf16[512,128]{1,0:T(8,128)(2,1)} %w_hbm.1), custom_call_target="tpu_custom_call" | custom-call | tf_op jit(solution)/shard_map/butterfly/pallas_call | solution.py:295
  127.4 2.3 %copy.8 = bf16[128,4096]{1,0:T(8,128)(2,1)} copy(bf16[128,4096]{1,0:T(8,128)(2,1)} %butterfly.1) | data formatting | bytes 2097152

commit v2 on v1

--- a/solution.py
+++ b/solution.py
@@ -28,8 +28,8 @@
 def kernel(
     q_hbm, k_hbm, v_hbm, pairs_ref, pos_ref, w_hbm, out_ref,
     q_ref, kv_own, kv_in, g_ref, w_own, w_sib, s_ref, p_ref, att_ref, att_in,
-    p_send, r1a, r1b, r2a, r2b, acc_ref,
-    load_sem, kv_ssem, kv_rsem, g_ssem, g_rsem, zu_s, zu_r, zd_s, zd_r,
+    p_send, r1a, r1b, r2a, r2b, acc_ref, pick_ref,
+    load_sem, kv_s, kv_r, g_ssem, g_rsem, zu_s, zu_r, zd_s, zd_r,
     yu_s, yu_r, yd_s, yd_r, far_s, far_r, sib_s, sib_r, att_s, att_r,
     one_s, one_r, two_s, two_r,
 ):
@@ -47,7 +47,11 @@
     sibling = (ctx, flip(head, 1))
     xu = (ctx, ((x + 1) % NX) * 2 + core)
     xd = (ctx, ((x + NX - 1) % NX) * 2 + core)
-    partners = (at(z, flip(y, 1)), yf, at(flip(z, 1), y), at(flip(z, 2), y), at((z + 4) % NZ, y))
+    z_far = (z + 4) % NZ
+    z1, z2, z4 = at(flip(z, 1), y), at(flip(z, 2), y), at(z_far, y)
+    z3, z6 = at(flip(flip(z, 1), 2), y), at(flip(z_far, 2), y)
+    y1, y3 = at(z, flip(y, 1)), at(z, flip((y + 2) % NY, 1))
+    inner = ((z + 1) // 2) % 2 == 1
 
     loads = [
         pltpu.make_async_copy(w_hbm, w_own.at[y, z], load_sem.at[0]),
@@ -59,20 +63,23 @@
         load.start()
 
     barrier = pltpu.get_barrier_semaphore()
-    peers = (zu, zd, yu, yd, yf, partners[3], partners[4], sibling, xu, xd)
+    peers = (zu, zd, yu, yd, yf, z2, z6, z4, sibling, xu, xd)
     for peer in peers:
         pl.semaphore_signal(barrier, inc=1, device_id=peer, device_id_type=MESH)
     pl.semaphore_wait(barrier, len(peers))
 
     sent = []
 
-    def send(src, dst, ssem, rsem, device):
+    def send(src, dst, ssem, rsem, device, where=None):
         copy = pltpu.make_async_remote_copy(
             src_ref=src, dst_ref=dst, send_sem=ssem, recv_sem=rsem,
             device_id=device, device_id_type=MESH,
         )
-        copy.start()
-        sent.append(copy)
+        if where is None:
+            copy.start()
+        else:
+            pl.when(where)(copy.start)
+        sent.append((copy, where))
 
     def arrived(dst, rsem):
         pltpu.make_async_copy(dst, dst, rsem).wait()
@@ -111,52 +118,76 @@
         if e % 2 == 1:
             send(high, high, far_s.at[e], far_r.at[e], yd)
 
-    def share(n, yy):
-        send(w_own.at[yy], w_sib.at[yy], sib_s.at[n], sib_r.at[n], sibling)
-
-    def kv_send(s):
-        i = (x + ORDER[s]) % NX
-        for n in (4, 3, 2, 1, 0):
-            send(kv_own.at[i], kv_in.at[n, i], kv_ssem.at[n, s], kv_rsem.at[n, s], partners[n])
-
-    loads[0].wait()
-    z_step(0)
-    loads[1].wait()
-    loads[2].wait()
-    kv_send(0)
-
-    wanted = pos_ref[pl.ds(ctx, 1), :]
+    def far_step(e):
+        arrived(w_own.at[y_far, slots[e]], far_r.at[e])
+        send(w_own.at[:, slots[e]], w_sib.at[:, slots[e]], sib_s.at[e], sib_r.at[e], sibling)
+
+    def chunk(s):
+        return (x + ORDER[s]) % NX
+
+    def kv_own_send(s):
+        i = chunk(s)
+        mine = kv_own.at[i]
+        send(mine, kv_in.at[3, i], kv_s.at[1, s], kv_r.at[3, s], z2, inner)
+        send(mine, kv_in.at[2, i], kv_s.at[0, s], kv_r.at[2, s], z1)
+        send(mine, kv_in.at[0, i], kv_s.at[2, s], kv_r.at[0, s], y1)
+
+    def kv_relay1(s):
+        i = chunk(s)
+        near = kv_in.at[2, i]
+        arrived(near, kv_r.at[2, s])
+        send(near, kv_in.at[3, i], kv_s.at[3, s], kv_r.at[3, s], z3, inner)
+        near = kv_in.at[0, i]
+        arrived(near, kv_r.at[0, s])
+        send(near, kv_in.at[1, i], kv_s.at[5, s], kv_r.at[1, s], y3)
+
+    def kv_relay2(s):
+        i = chunk(s)
+        mid = kv_in.at[3, i]
+        arrived(mid, kv_r.at[3, s])
+        send(mid, kv_in.at[4, i], kv_s.at[4, s], kv_r.at[4, s], z6)
+
+    def kv_wait(s):
+        i = chunk(s)
+        for n in (1, 4):
+            arrived(kv_in.at[n, i], kv_r.at[n, s])
+
     zpos = z // 4 + 2 * ((z // 2) % 2) + 4 * (z % 2)
-    for part in range(2):
-        picked = jnp.zeros((PICK, HD), jnp.float32)
-        for i in range(CHUNKS):
-            spot = lax.broadcasted_iota(jnp.int32, (ROWS, PICK), 0) + (ctx * 1024 + i * ROWS)
-            chosen = (spot == wanted).astype(jnp.float32).astype(jnp.bfloat16)
-            picked += lax.dot_general(
-                chosen, kv_own[i, part], (((0,), (0,)), ((), ())),
-                preferred_element_type=jnp.float32,
-            )
-        g_ref[part, y, pl.ds(pl.multiple_of(zpos * PICK, PICK), PICK), :] = picked.astype(jnp.bfloat16)
+
+    def pick():
+        wanted = pos_ref[pl.ds(ctx // 4, 1), :]
+        for part in range(2):
+            picked = jnp.zeros((4 * PICK, HD), jnp.float32)
+            for i in range(CHUNKS):
+                spot = lax.broadcasted_iota(jnp.int32, (ROWS, 4 * PICK), 0) + (ctx * 1024 + i * ROWS)
+                chosen = (spot == wanted).astype(jnp.float32).astype(jnp.bfloat16)
+                picked += lax.dot_general(
+                    chosen, kv_own[i, part], (((0,), (0,)), ((), ())),
+                    preferred_element_type=jnp.float32,
+                )
+            pick_ref[...] = picked
+            mine = pick_ref[pl.ds(pl.multiple_of((ctx % 4) * PICK, PICK), PICK), :]
+            g_ref[part, y, pl.ds(pl.multiple_of(zpos * PICK, PICK), PICK), :] = mine.astype(jnp.bfloat16)
 
     def g_rows(yy, size, slot):
         start = (slot // size) * size * PICK
         return g_ref.at[:, yy, pl.ds(pl.multiple_of(start, size * PICK), size * PICK), :]
 
-    for n, partner in enumerate((partners[4], partners[3], partners[2])):
-        size = 1 << n
-        mine = g_rows(y, size, zpos)
-        send(mine, mine, g_ssem.at[n], g_rsem.at[n], partner)
-        arrived(g_rows(y, size, flip(zpos, size)), g_rsem.at[n])
-        if n < 2:
-            z_step(n + 1)
-    whole = g_ref.at[:, y]
-    for n, peer in enumerate((yu, yd, yf)):
-        send(whole, whole, g_ssem.at[3 + n], g_rsem.at[3 + n], peer)
-    kv_send(1)
-    z_step(3)
-    for n, yy in enumerate((y_dn, y_up, y_far)):
-        arrived(g_ref.at[:, yy], g_rsem.at[3 + n])
-    loads[3].wait()
+    def g_send(n):
+        mine = g_rows(y, 1 << n, zpos)
+        send(mine, mine, g_ssem.at[n], g_rsem.at[n], (z4, z2, z1)[n])
+
+    def g_wait(n):
+        arrived(g_rows(y, 1 << n, flip(zpos, 1 << n)), g_rsem.at[n])
+
+    def g_y_send():
+        whole = g_ref.at[:, y]
+        for n, peer in enumerate((yu, yd, yf)):
+            send(whole, whole, g_ssem.at[3 + n], g_rsem.at[3 + n], peer)
+
+    def g_y_wait():
+        for n, yy in enumerate((y_dn, y_up, y_far)):
+            arrived(g_ref.at[:, yy], g_rsem.at[3 + n])
 
     def attend(i, t):
         j = 2 * i + t
@@ -206,37 +237,14 @@
         for h in range(GROUPS):
             att_ref[i, t, :, h * HD : (h + 1) * HD] = result[h * BLK : (h + 1) * BLK]
 
-    for s in range(CHUNKS):
-        i = (x + ORDER[s]) % NX
-        for n in range(5):
-            arrived(kv_in.at[n, i], kv_rsem.at[n, s])
-        for t in range(2):
-            attend(i, t)
+    def pass_on(s):
+        i = chunk(s)
         send(att_ref.at[i, 1 - core], att_in.at[i], att_s.at[s], att_r.at[s], sibling)
-        if s == 0:
-            kv_send(2)
-            z_step(4)
-            share(0, y)
-            for e in range(4):
-                y_step(e)
-        if s == 1:
-            kv_send(3)
-            for e in range(4, 8):
-                y_step(e)
-            share(1, y_dn)
-            share(2, y_up)
-        if s == 2:
-            for e in range(8):
-                arrived(w_own.at[y_far, slots[e]], far_r.at[e])
-            share(3, y_far)
-
-    for n, yy in enumerate((y, y_up, y_dn, y_far)):
-        arrived(w_sib.at[yy], sib_r.at[(0, 2, 1, 3)[n]])
-
-    def project(i, q, extra, put):
+
+    def project(i, e, extra, put):
         left, right = att_ref[i, core], att_in[i]
-        for half in range(4):
-            zz, yy = 2 * q + half // 2, 2 * (half % 2)
+        for half in range(2):
+            zz, yy = slots[e], 2 * half
             columns = slice(half * 256, half * 256 + 256)
             total = jnp.dot(
                 left, jnp.concatenate([w_own[yy, zz], w_own[yy + 1, zz]], axis=1),
@@ -249,43 +257,147 @@
                 total = total + extra[:, columns].astype(jnp.float32)
             put(columns, total)
 
-    def project_send(n, i, q, extra, dst, ssem, rsem, device):
+    def project_send(n, i, e, extra, dst, ssem, rsem, device):
         def put(columns, total):
-            p_send[n, q, :, columns] = total.astype(jnp.bfloat16)
-
-        project(i, q, extra, put)
-        send(p_send.at[n, q], dst, ssem, rsem, device)
-
-    for s in range(CHUNKS):
-        i = (x + ORDER[s]) % NX
-        arrived(att_in.at[i], att_r.at[s])
-    far, up, down = (x + 2) % NX, (x + 1) % NX, (x + 3) % NX
-    for q in (0, 2, 1, 3):
-        dst, device = (r1a.at[q], xu) if q < 2 else (r1b.at[q - 2], xd)
-        project_send(0, far, q, None, dst, one_s.at[q], one_r.at[q], device)
-    for q in (2, 3):
-        project_send(1, up, q, None, r2a.at[q], two_s.at[q], two_r.at[q], xu)
-        project_send(2, down, q - 2, None, r2b.at[q - 2], two_s.at[q + 2], two_r.at[q + 2], xd)
-    for q in (0, 1):
-        arrived(r1a.at[q], one_r.at[q])
-        project_send(1, up, q, r1a.at[q], r2a.at[q], two_s.at[q], two_r.at[q], xu)
-        arrived(r1b.at[q], one_r.at[q + 2])
-        project_send(2, down, q + 2, r1b.at[q], r2b.at[q + 2], two_s.at[q + 6], two_r.at[q + 6], xd)
-
-    for q in range(4):
-
-        def put(columns, total, q=q):
-            acc_ref[q, :, columns] = total
-
-        project(x, q, None, put)
-    for q in (2, 0, 3, 1):
-        arrived(r2a.at[q], two_r.at[q])
-        arrived(r2b.at[q], two_r.at[q + 4])
-        out_ref[:, q * 1024 : q * 1024 + 1024] = (
-            acc_ref[q] + r2a[q].astype(jnp.float32) + r2b[q].astype(jnp.float32)
+            p_send[n, e, :, columns] = total.astype(jnp.bfloat16)
+
+        project(i, e, extra, put)
+        send(p_send.at[n, e], dst, ssem, rsem, device)
+
+    def w_wait(e):
+        arrived(w_sib.at[:, slots[e]], sib_r.at[e])
+
+    def att_wait(s):
+        arrived(att_in.at[chunk(s)], att_r.at[s])
+
+    def p_far(e):
+        dst, device = (r1a, xu) if e % 2 == 0 else (r1b, xd)
+        project_send(0, chunk(0), e, None, dst.at[e // 2], one_s.at[e], one_r.at[e], device)
+
+    def p_up(e):
+        extra = None
+        if e % 2 == 0:
+            extra = r1a.at[e // 2]
+            arrived(extra, one_r.at[e])
+        project_send(1, chunk(1), e, extra, r2a.at[e], two_s.at[e], two_r.at[e], xu)
+
+    def p_down(e):
+        extra = None
+        if e % 2 == 1:
+            extra = r1b.at[e // 2]
+            arrived(extra, one_r.at[e])
+        project_send(2, chunk(2), e, extra, r2b.at[e], two_s.at[8 + e], two_r.at[8 + e], xd)
+
+    def p_mine(e):
+        def put(columns, total):
+            acc_ref[e, :, columns] = total
+
+        project(chunk(3), e, None, put)
+
+    def finish(e):
+        arrived(r2a.at[e], two_r.at[e])
+        arrived(r2b.at[e], two_r.at[8 + e])
+        columns = pl.ds(pl.multiple_of(slots[e] * 512, 512), 512)
+        out_ref[:, columns] = (
+            acc_ref[e] + r2a[e].astype(jnp.float32) + r2b[e].astype(jnp.float32)
         ).astype(jnp.bfloat16)
-    for copy in sent:
-        copy.wait_send()
+
+    def attend_step(s, t):
+        attend(chunk(s), t)
+
+    loads[0].wait()
+    z_step(0)
+    loads[1].wait()
+    loads[2].wait()
+    kv_own_send(0)
+    pick()
+    g_send(0)
+    kv_relay1(0)
+    g_wait(0)
+    g_send(1)
+    z_step(1)
+    kv_own_send(1)
+    kv_relay2(0)
+    g_wait(1)
+    g_send(2)
+    z_step(2)
+    g_wait(2)
+    g_y_send()
+    z_step(3)
+    kv_relay1(1)
+    z_step(4)
+    y_step(0)
+    y_step(1)
+    kv_wait(0)
+    g_y_wait()
+    loads[3].wait()
+    kv_own_send(2)
+    attend_step(0, 0)
+    kv_relay2(1)
+    y_step(2)
+    attend_step(0, 1)
+    pass_on(0)
+    y_step(3)
+    kv_relay1(2)
+    kv_wait(1)
+    kv_own_send(3)
+    attend_step(1, 0)
+    kv_relay2(2)
+    y_step(4)
+    far_step(0)
+    far_step(1)
+    attend_step(1, 1)
+    pass_on(1)
+    kv_relay1(3)
+    y_step(5)
+    att_wait(0)
+    far_step(2)
+    for e in range(2):
+        w_wait(e)
+        p_far(e)
+    y_step(6)
+    y_step(7)
+    far_step(3)
+    kv_relay2(3)
+    kv_wait(2)
+    attend_step(2, 0)
+    far_step(4)
+    for e in range(2, 4):
+        w_wait(e)
+        p_far(e)
+    attend_step(2, 1)
+    pass_on(2)
+    far_step(5)
+    far_step(6)
+    far_step(7)
+    for e in range(4, 8):
+        w_wait(e)
+        p_far(e)
+    att_wait(1)
+    att_wait(2)
+    for e in range(4):
+        p_up(2 * e + 1)
+        p_down(2 * e)
+    for e in range(2):
+        p_up(2 * e)
+        p_down(2 * e + 1)
+    kv_wait(3)
+    attend_step(3, 0)
+    for e in range(2, 4):
+        p_up(2 * e)
+        p_down(2 * e + 1)
+    attend_step(3, 1)
+    pass_on(3)
+    att_wait(3)
+    for e in range(8):
+        p_mine(e)
+    for e in (1, 0, 3, 2, 5, 4, 7, 6):
+        finish(e)
+    for copy, where in sent:
+        if where is None:
+            copy.wait_send()
+        else:
+            pl.when(where)(copy.wait_send)
 
 
 def shards(queries, keys, values, pairs, positions, w_out):
@@ -313,17 +425,18 @@
             pltpu.VMEM((GROUPS * BLK, KEYS), bf16),
             pltpu.VMEM((CHUNKS, 2, BLK, GROUPS * HD), bf16),
             pltpu.VMEM((CHUNKS, BLK, GROUPS * HD), bf16),
-            pltpu.VMEM((3, 4, BLK, 1024), bf16),
-            pltpu.VMEM((2, BLK, 1024), bf16),
-            pltpu.VMEM((2, BLK, 1024), bf16),
-            pltpu.VMEM((4, BLK, 1024), bf16),
-            pltpu.VMEM((4, BLK, 1024), bf16),
-            pltpu.VMEM((4, BLK, 1024), f32),
-            dma((4,)), dma((5, CHUNKS)), dma((5, CHUNKS)), dma((6,)), dma((6,)),
+            pltpu.VMEM((3, 8, BLK, 512), bf16),
+            pltpu.VMEM((4, BLK, 512), bf16),
+            pltpu.VMEM((4, BLK, 512), bf16),
+            pltpu.VMEM((8, BLK, 512), bf16),
+            pltpu.VMEM((8, BLK, 512), bf16),
+            pltpu.VMEM((8, BLK, 512), f32),
+            pltpu.VMEM((4 * PICK, HD), f32),
+            dma((4,)), dma((6, CHUNKS)), dma((5, CHUNKS)), dma((6,)), dma((6,)),
             dma((4,)), dma((4,)), dma((3,)), dma((3,)),
             dma((8,)), dma((8,)), dma((8,)), dma((8,)), dma((8,)), dma((8,)),
-            dma((4,)), dma((4,)), dma((4,)), dma((4,)),
-            dma((4,)), dma((4,)), dma((8,)), dma((8,)),
+            dma((8,)), dma((8,)), dma((4,)), dma((4,)),
+            dma((8,)), dma((8,)), dma((16,)), dma((16,)),
         ],
         compiler_params=pltpu.CompilerParams(
             collective_id=0, has_side_effects=True, vmem_limit_bytes=56 * 2**20
@@ -334,7 +447,7 @@
         keys.reshape(CHUNKS, ROWS, HD),
         values.reshape(CHUNKS, ROWS, HD),
         pairs,
-        positions.reshape(NY * NZ, PICK),
+        positions.reshape(BLOCKS, NY * NZ * PICK // BLOCKS),
         w_out,
     )
 

time: 130 us -> 111 us (0.85)
  Pallas kernels: 126 us -> 108 us
  local copies, waits for them, and re-layouts: 3.65 us -> 2.29 us
    pallas_call x1, Pallas kernels: 126 us -> 108 us  [shards(): pl.pallas_call(kernel, out_shape=jax.ShapeDtypeStruct((BLK, 4096), bf16),...]
    reshape x1 -> x0, local copies, waits for them, and re-layouts: 1.36 us -> none  [shards(): positions.reshape(NY * NZ, PICK)]
where the time goes in v2:
time: 111 us; the launch traced here: 110 us
  Pallas kernels  108 us (97%)
  local copies, waits for them, and re-layouts  2.29 us (2%)
    pallas_call x1, Pallas kernels, shards(): pl.pallas_call(kernel, out_shape=jax.ShapeDtypeStruct((BLK, 4096), bf16),...  108 us
    unnamed x1, local copies, waits for them, and re-layouts  2.29 us

profile of v2, /device:TPU:1, one launch (start us, length us, event | category | flops | bytes accessed | tf_op | source)
XLA Modules:
  0.0 109.8 jit_solution(7985152543147382)
XLA Ops:
  0.0 107.5 %butterfly.1 = bf16[128,4096]{1,0:T(8,128)(2,1)} custom-call(bf16[1024,512]{1,0:T(8,128)(2,1)} %q_hbm.1, bf16[4,256,128]{2,1,0:T(8,128)(2,1)} %bitcast.3, bf16[4,256,128]{2,1,0:T(8,128)(2,1)} %bitcast.4, s32[8,8]{1,0:T(8,128)} %pairs_ref.1, s32[8,128]{1,0:T(8,128)} %bitcast.5, bf16[512,128]{1,0:T(8,128)(2,1)} %w_hbm.1), custom_call_target="tpu_custom_call" | custom-call | tf_op jit(solution)/shard_map/butterfly/pallas_call | solution.py:407
  107.5 2.3 %copy.8 = bf16[128,4096]{1,0:T(8,128)(2,1)} copy(bf16[128,4096]{1,0:T(8,128)(2,1)} %butterfly.1) | data formatting | bytes 2097152

commit v3 on v2

--- a/solution.py
+++ b/solution.py
@@ -48,8 +48,10 @@
     xu = (ctx, ((x + 1) % NX) * 2 + core)
     xd = (ctx, ((x + NX - 1) % NX) * 2 + core)
     z_far = (z + 4) % NZ
-    z1, z2, z4 = at(flip(z, 1), y), at(flip(z, 2), y), at(z_far, y)
+    z1, z2 = at(flip(z, 1), y), at(flip(z, 2), y)
     z3, z6 = at(flip(flip(z, 1), 2), y), at(flip(z_far, 2), y)
+    along = [(k, (z + k) % NZ) for k in (1, 7, 2, 6, 3, 5, 4)]
+    zu2, zd2 = at((z + 2) % NZ, y), at((z + 6) % NZ, y)
     y1, y3 = at(z, flip(y, 1)), at(z, flip((y + 2) % NY, 1))
     inner = ((z + 1) // 2) % 2 == 1
 
@@ -63,7 +65,7 @@
         load.start()
 
     barrier = pltpu.get_barrier_semaphore()
-    peers = (zu, zd, yu, yd, yf, z2, z6, z4, sibling, xu, xd)
+    peers = [at(zz, y) for _, zz in along] + [yu, yd, yf, sibling, xu, xd]
     for peer in peers:
         pl.semaphore_signal(barrier, inc=1, device_id=peer, device_id_type=MESH)
     pl.semaphore_wait(barrier, len(peers))
@@ -91,29 +93,28 @@
         send(ref, ref, yu_s.at[e], yu_r.at[e], yu)
         send(ref, ref, yd_s.at[e], yd_r.at[e], yd)
 
-    def z_step(t):
+    def z_forth(t):
+        ref = w_own.at[y, z if t == 0 else slots[2 * t - 1]]
         if t > 0:
-            arrived(w_own.at[y, slots[2 * t - 1]], zu_r.at[t - 1])
+            arrived(ref, zu_r.at[t - 1])
         if t < 4:
-            ref = w_own.at[y, z if t == 0 else slots[2 * t - 1]]
             send(ref, ref, zu_s.at[t], zu_r.at[t], zu)
-        if 0 < t < 4:
-            arrived(w_own.at[y, slots[2 * t]], zd_r.at[t - 1])
+
+    def z_back(t):
+        ref = w_own.at[y, slots[2 * t]]
+        if t > 0:
+            arrived(ref, zd_r.at[t - 1])
         if t < 3:
-            ref = w_own.at[y, slots[2 * t]]
             send(ref, ref, zd_s.at[t], zd_r.at[t], zd)
-        if t == 0:
-            spread(0)
-        else:
-            spread(2 * t - 1)
-            if t < 4:
-                spread(2 * t)
-
-    def y_step(e):
-        low, high = w_own.at[y_dn, slots[e]], w_own.at[y_up, slots[e]]
+
+    def y_low(e):
+        low = w_own.at[y_dn, slots[e]]
         arrived(low, yu_r.at[e])
         if e % 2 == 0:
             send(low, low, far_s.at[e], far_r.at[e], yu)
+
+    def y_high(e):
+        high = w_own.at[y_up, slots[e]]
         arrived(high, yd_r.at[e])
         if e % 2 == 1:
             send(high, high, far_s.at[e], far_r.at[e], yd)
@@ -125,18 +126,24 @@
     def chunk(s):
         return (x + ORDER[s]) % NX
 
-    def kv_own_send(s):
+    def kv_own_z(s):
         i = chunk(s)
         mine = kv_own.at[i]
         send(mine, kv_in.at[3, i], kv_s.at[1, s], kv_r.at[3, s], z2, inner)
         send(mine, kv_in.at[2, i], kv_s.at[0, s], kv_r.at[2, s], z1)
-        send(mine, kv_in.at[0, i], kv_s.at[2, s], kv_r.at[0, s], y1)
-
-    def kv_relay1(s):
+
+    def kv_own_y(s):
+        i = chunk(s)
+        send(kv_own.at[i], kv_in.at[0, i], kv_s.at[2, s], kv_r.at[0, s], y1)
+
+    def kv_relay_z(s):
         i = chunk(s)
         near = kv_in.at[2, i]
         arrived(near, kv_r.at[2, s])
         send(near, kv_in.at[3, i], kv_s.at[3, s], kv_r.at[3, s], z3, inner)
+
+    def kv_relay_y(s):
+        i = chunk(s)
         near = kv_in.at[0, i]
         arrived(near, kv_r.at[0, s])
         send(near, kv_in.at[1, i], kv_s.at[5, s], kv_r.at[1, s], y3)
@@ -147,12 +154,11 @@
         arrived(mid, kv_r.at[3, s])
         send(mid, kv_in.at[4, i], kv_s.at[4, s], kv_r.at[4, s], z6)
 
-    def kv_wait(s):
-        i = chunk(s)
-        for n in (1, 4):
-            arrived(kv_in.at[n, i], kv_r.at[n, s])
-
-    zpos = z // 4 + 2 * ((z // 2) % 2) + 4 * (z % 2)
+    def kv_wait_y(s):
+        arrived(kv_in.at[1, chunk(s)], kv_r.at[1, s])
+
+    def kv_wait_z(s):
+        arrived(kv_in.at[4, chunk(s)], kv_r.at[4, s])
 
     def pick():
         wanted = pos_ref[pl.ds(ctx // 4, 1), :]
@@ -167,27 +173,27 @@
                 )
             pick_ref[...] = picked
             mine = pick_ref[pl.ds(pl.multiple_of((ctx % 4) * PICK, PICK), PICK), :]
-            g_ref[part, y, pl.ds(pl.multiple_of(zpos * PICK, PICK), PICK), :] = mine.astype(jnp.bfloat16)
-
-    def g_rows(yy, size, slot):
-        start = (slot // size) * size * PICK
-        return g_ref.at[:, yy, pl.ds(pl.multiple_of(start, size * PICK), size * PICK), :]
-
-    def g_send(n):
-        mine = g_rows(y, 1 << n, zpos)
-        send(mine, mine, g_ssem.at[n], g_rsem.at[n], (z4, z2, z1)[n])
-
-    def g_wait(n):
-        arrived(g_rows(y, 1 << n, flip(zpos, 1 << n)), g_rsem.at[n])
+            g_ref[part, y, pl.ds(pl.multiple_of(z * PICK, PICK), PICK), :] = mine.astype(jnp.bfloat16)
+
+    def g_rows(zz):
+        return g_ref.at[:, y, pl.ds(pl.multiple_of(zz * PICK, PICK), PICK), :]
+
+    def g_send():
+        for k, zz in along:
+            send(g_rows(z), g_rows(z), g_ssem.at[2 + k], g_rsem.at[2 + k], at(zz, y))
+
+    def g_wait():
+        for k, _ in along:
+            arrived(g_rows((z + NZ - k) % NZ), g_rsem.at[2 + k])
 
     def g_y_send():
         whole = g_ref.at[:, y]
         for n, peer in enumerate((yu, yd, yf)):
-            send(whole, whole, g_ssem.at[3 + n], g_rsem.at[3 + n], peer)
+            send(whole, whole, g_ssem.at[n], g_rsem.at[n], peer)
 
     def g_y_wait():
         for n, yy in enumerate((y_dn, y_up, y_far)):
-            arrived(g_ref.at[:, yy], g_rsem.at[3 + n])
+            arrived(g_ref.at[:, yy], g_rsem.at[n])
 
     def attend(i, t):
         j = 2 * i + t
@@ -197,7 +203,7 @@
             if n < 4:
                 jj = own[n]
                 return kv_own[jj // 2, part, pl.ds(pl.multiple_of((jj % 2) * BLK, BLK), BLK), :]
-            return kv_in[n - 4, i, part, pl.ds(t * BLK, BLK), :]
+            return kv_in[n - 4, i, part, pl.ds(pl.multiple_of(t * BLK, BLK), BLK), :]
 
         rows = pl.ds(pl.multiple_of(j * BLK, BLK), BLK)
         queries = jnp.concatenate(
@@ -302,97 +308,151 @@
             acc_ref[e] + r2a[e].astype(jnp.float32) + r2b[e].astype(jnp.float32)
         ).astype(jnp.bfloat16)
 
-    def attend_step(s, t):
-        attend(chunk(s), t)
-
-    loads[0].wait()
-    z_step(0)
+    def attend_first(s):
+        attend(chunk(s), 1 - core)
+        pass_on(s)
+
+    def attend_last(s):
+        attend(chunk(s), core)
+
     loads[1].wait()
     loads[2].wait()
-    kv_own_send(0)
+    kv_own_y(1)
+    loads[0].wait()
+    z_forth(0)
+    z_back(0)
+    spread(0)
     pick()
-    g_send(0)
-    kv_relay1(0)
-    g_wait(0)
-    g_send(1)
-    z_step(1)
-    kv_own_send(1)
+    g_send()
+    z_forth(1)
+    z_back(1)
+    kv_own_y(0)
+    spread(1)
+    spread(2)
+    z_forth(2)
+    y_high(0)
+    kv_own_z(0)
+    spread(3)
+    z_back(2)
+    g_wait()
+    y_high(1)
+    g_y_send()
+    kv_relay_y(1)
+    z_forth(3)
+    y_low(3)
+    z_forth(4)
+    kv_relay_y(0)
+    y_high(3)
+    kv_relay_z(0)
+    kv_own_z(1)
+    y_high(2)
+    y_low(0)
+    kv_own_y(2)
+    kv_own_z(2)
     kv_relay2(0)
-    g_wait(1)
-    g_send(2)
-    z_step(2)
-    g_wait(2)
-    g_y_send()
-    z_step(3)
-    kv_relay1(1)
-    z_step(4)
-    y_step(0)
-    y_step(1)
-    kv_wait(0)
+    spread(4)
+    spread(5)
+    kv_relay_z(1)
+    z_back(3)
+    kv_relay_z(2)
+    kv_wait_y(0)
+    y_low(2)
+    far_step(3)
+    y_low(1)
+    kv_relay_y(2)
+    kv_relay2(1)
+    far_step(0)
+    spread(7)
+    y_high(5)
+    spread(6)
+    w_wait(3)
+    far_step(1)
+    kv_wait_z(0)
     g_y_wait()
+    y_low(4)
+    kv_wait_y(1)
     loads[3].wait()
-    kv_own_send(2)
-    attend_step(0, 0)
-    kv_relay2(1)
-    y_step(2)
-    attend_step(0, 1)
-    pass_on(0)
-    y_step(3)
-    kv_relay1(2)
-    kv_wait(1)
-    kv_own_send(3)
-    attend_step(1, 0)
+    attend_first(0)
+    kv_own_y(3)
+    attend_last(0)
+    att_wait(0)
+    kv_wait_z(1)
+    w_wait(1)
     kv_relay2(2)
-    y_step(4)
-    far_step(0)
-    far_step(1)
-    attend_step(1, 1)
-    pass_on(1)
-    kv_relay1(3)
-    y_step(5)
-    att_wait(0)
+    y_low(5)
     far_step(2)
-    for e in range(2):
-        w_wait(e)
-        p_far(e)
-    y_step(6)
-    y_step(7)
-    far_step(3)
+    w_wait(0)
+    attend_first(1)
+    p_far(0)
+    p_far(3)
+    far_step(5)
+    p_far(1)
+    w_wait(2)
+    p_far(2)
+    kv_own_z(3)
+    attend_last(1)
+    y_high(7)
+    y_low(6)
+    kv_wait_y(2)
+    w_wait(5)
+    y_high(6)
+    kv_wait_z(2)
+    y_high(4)
+    att_wait(1)
+    p_up(5)
+    p_far(5)
+    attend_first(2)
+    kv_relay_z(3)
+    far_step(4)
+    y_low(7)
+    attend_last(2)
+    p_up(3)
+    att_wait(2)
+    far_step(6)
+    p_down(2)
+    p_down(3)
+    kv_relay_y(3)
     kv_relay2(3)
-    kv_wait(2)
-    attend_step(2, 0)
-    far_step(4)
-    for e in range(2, 4):
-        w_wait(e)
-        p_far(e)
-    attend_step(2, 1)
-    pass_on(2)
-    far_step(5)
-    far_step(6)
     far_step(7)
-    for e in range(4, 8):
-        w_wait(e)
-        p_far(e)
-    att_wait(1)
-    att_wait(2)
-    for e in range(4):
-        p_up(2 * e + 1)
-        p_down(2 * e)
-    for e in range(2):
-        p_up(2 * e)
-        p_down(2 * e + 1)
-    kv_wait(3)
-    attend_step(3, 0)
-    for e in range(2, 4):
-        p_up(2 * e)
-        p_down(2 * e + 1)
-    attend_step(3, 1)
-    pass_on(3)
+    p_up(0)
+    w_wait(6)
+    w_wait(4)
+    w_wait(7)
+    p_far(4)
+    p_far(7)
+    p_far(6)
+    kv_wait_y(3)
+    p_down(0)
+    p_up(1)
+    p_down(1)
+    kv_wait_z(3)
+    attend_first(3)
+    attend_last(3)
+    p_up(2)
     att_wait(3)
-    for e in range(8):
-        p_mine(e)
-    for e in (1, 0, 3, 2, 5, 4, 7, 6):
-        finish(e)
+    p_up(6)
+    p_up(7)
+    p_down(5)
+    p_mine(3)
+    p_up(4)
+    p_mine(0)
+    p_down(7)
+    p_mine(1)
+    finish(3)
+    p_mine(4)
+    p_mine(6)
+    p_down(6)
+    p_mine(2)
+    p_down(4)
+    finish(2)
+    p_mine(7)
+    finish(7)
+    finish(0)
+    p_mine(5)
+    finish(1)
+    finish(6)
+    finish(5)
+    finish(4)
     for copy, where in sent:
         if where is None:
             copy.wait_send()
@@ -432,8 +492,8 @@
             pltpu.VMEM((8, BLK, 512), bf16),
             pltpu.VMEM((8, BLK, 512), f32),
             pltpu.VMEM((4 * PICK, HD), f32),
-            dma((4,)), dma((6, CHUNKS)), dma((5, CHUNKS)), dma((6,)), dma((6,)),
-            dma((4,)), dma((4,)), dma((3,)), dma((3,)),
+            dma((4,)), dma((6, CHUNKS)), dma((5, CHUNKS)), dma((10,)), dma((10,)),
+            dma((4,)), dma((4,)), dma((4,)), dma((4,)),
             dma((8,)), dma((8,)), dma((8,)), dma((8,)), dma((8,)), dma((8,)),
             dma((8,)), dma((8,)), dma((4,)), dma((4,)),
             dma((8,)), dma((8,)), dma((16,)), dma((16,)),

time: 111 us -> 101 us (0.910)
  Pallas kernels: 108 us -> 98 us
    pallas_call x1, Pallas kernels: 108 us -> 98 us  [shards(): pl.pallas_call(kernel, out_shape=jax.ShapeDtypeStruct((BLK, 4096), bf16),...]
where the time goes in v3:
time: 101 us; the launch traced here: 100 us
  Pallas kernels  98 us (97%)
  local copies, waits for them, and re-layouts  2.29 us (2%)
    pallas_call x1, Pallas kernels, shards(): pl.pallas_call(kernel, out_shape=jax.ShapeDtypeStruct((BLK, 4096), bf16),...  98 us
    unnamed x1, local copies, waits for them, and re-layouts  2.29 us

profile of v3, /device:TPU:1, one launch (start us, length us, event | category | flops | bytes accessed | tf_op | source)
XLA Modules:
  0.0 100.3 jit_solution(15853769292739317246)
XLA Ops:
  0.0 98.0 %butterfly.1 = bf16[128,4096]{1,0:T(8,128)(2,1)} custom-call(bf16[1024,512]{1,0:T(8,128)(2,1)} %q_hbm.1, bf16[4,256,128]{2,1,0:T(8,128)(2,1)} %bitcast.3, bf16[4,256,128]{2,1,0:T(8,128)(2,1)} %bitcast.4, s32[8,8]{1,0:T(8,128)} %pairs_ref.1, s32[8,128]{1,0:T(8,128)} %bitcast.5, bf16[512,128]{1,0:T(8,128)(2,1)} %w_hbm.1), custom_call_target="tpu_custom_call" | custom-call | tf_op jit(solution)/shard_map/butterfly/pallas_call | solution.py:467
  98.0 2.3 %copy.8 = bf16[128,4096]{1,0:T(8,128)(2,1)} copy(bf16[128,4096]{1,0:T(8,128)(2,1)} %butterfly.1) | data formatting | bytes 2097152

commit v4 on v3

--- a/solution.py
+++ b/solution.py
@@ -82,6 +82,15 @@
         else:
             pl.when(where)(copy.start)
         sent.append((copy, where))
+
+    def settle(keep):
+        done = len(sent) - keep
+        for copy, where in sent[:done]:
+            if where is None:
+                copy.wait_send()
+            else:
+                pl.when(where)(copy.wait_send)
+        del sent[:done]
 
     def arrived(dst, rsem):
         pltpu.make_async_copy(dst, dst, rsem).wait()
@@ -315,149 +324,146 @@
     def attend_last(s):
         attend(chunk(s), core)
 
+    loads[0].wait()
+    z_forth(0)
     loads[1].wait()
     loads[2].wait()
     kv_own_y(1)
-    loads[0].wait()
-    z_forth(0)
     z_back(0)
-    spread(0)
     pick()
     g_send()
+    spread(0)
     z_forth(1)
     z_back(1)
+    spread(2)
+    spread(1)
+    y_low(0)
     kv_own_y(0)
-    spread(1)
-    spread(2)
+    kv_own_z(1)
+    kv_relay_y(1)
     z_forth(2)
-    y_high(0)
-    kv_own_z(0)
     spread(3)
-    z_back(2)
     g_wait()
     y_high(1)
+    z_back(2)
+    kv_own_z(0)
+    spread(4)
+    kv_relay_z(1)
     g_y_send()
-    kv_relay_y(1)
+    y_high(3)
+    y_high(0)
+    kv_own_z(2)
     z_forth(3)
+    kv_own_y(2)
+    kv_relay_y(0)
+    kv_relay_z(0)
+    kv_relay2(0)
+    kv_relay2(1)
+    z_back(3)
+    spread(5)
     y_low(3)
+    y_low(1)
+    y_high(4)
+    kv_relay_z(2)
     z_forth(4)
-    kv_relay_y(0)
-    y_high(3)
-    kv_relay_z(0)
-    kv_own_z(1)
-    y_high(2)
-    y_low(0)
-    kv_own_y(2)
-    kv_own_z(2)
-    kv_relay2(0)
-    spread(4)
-    spread(5)
-    kv_relay_z(1)
-    z_back(3)
-    kv_relay_z(2)
+    y_high(5)
+    kv_relay_y(2)
+    far_step(3)
+    kv_own_z(3)
+    y_low(2)
+    g_y_wait()
     kv_wait_y(0)
-    y_low(2)
-    far_step(3)
-    y_low(1)
-    kv_relay_y(2)
-    kv_relay2(1)
+    kv_wait_z(0)
+    far_step(1)
+    spread(6)
     far_step(0)
-    spread(7)
-    y_high(5)
-    spread(6)
-    w_wait(3)
-    far_step(1)
-    kv_wait_z(0)
-    g_y_wait()
-    y_low(4)
-    kv_wait_y(1)
+    kv_relay2(2)
     loads[3].wait()
     attend_first(0)
     kv_own_y(3)
+    w_wait(3)
+    y_low(5)
+    y_high(2)
+    spread(7)
     attend_last(0)
-    att_wait(0)
+    kv_wait_y(1)
     kv_wait_z(1)
     w_wait(1)
-    kv_relay2(2)
-    y_low(5)
-    far_step(2)
+    attend_first(1)
     w_wait(0)
-    attend_first(1)
+    far_step(5)
+    att_wait(0)
     p_far(0)
     p_far(3)
-    far_step(5)
+    attend_last(1)
+    att_wait(1)
+    kv_relay_z(3)
+    kv_wait_y(2)
+    kv_wait_z(2)
     p_far(1)
+    far_step(2)
+    y_low(4)
+    p_up(1)
+    y_high(6)
+    attend_first(2)
+    p_up(0)
+    y_high(7)
     w_wait(2)
+    w_wait(5)
+    y_low(6)
+    y_low(7)
+    p_far(5)
     p_far(2)
-    kv_own_z(3)
-    attend_last(1)
-    y_high(7)
-    y_low(6)
-    kv_wait_y(2)
-    w_wait(5)
-    y_high(6)
-    kv_wait_z(2)
-    y_high(4)
-    att_wait(1)
-    p_up(5)
-    p_far(5)
-    attend_first(2)
-    kv_relay_z(3)
+    attend_last(2)
+    kv_relay_y(3)
     far_step(4)
-    y_low(7)
-    attend_last(2)
+    att_wait(2)
+    p_down(3)
+    p_down(2)
     p_up(3)
-    att_wait(2)
+    kv_relay2(3)
+    w_wait(4)
     far_step(6)
-    p_down(2)
-    p_down(3)
-    kv_relay_y(3)
-    kv_relay2(3)
+    p_far(4)
+    p_down(5)
     far_step(7)
-    p_up(0)
+    p_up(2)
+    w_wait(7)
+    kv_wait_y(3)
     w_wait(6)
-    w_wait(4)
-    w_wait(7)
-    p_far(4)
+    p_down(4)
+    kv_wait_z(3)
+    attend_first(3)
     p_far(7)
     p_far(6)
-    kv_wait_y(3)
+    p_down(6)
+    p_up(4)
+    att_wait(3)
+    attend_last(3)
+    p_down(1)
+    p_up(7)
+    p_up(5)
+    p_mine(2)
+    p_mine(3)
+    finish(3)
+    p_mine(0)
+    p_mine(1)
+    p_mine(6)
+    p_up(6)
+    p_mine(4)
+    p_down(7)
     p_down(0)
-    p_up(1)
-    p_down(1)
-    kv_wait_z(3)
-    attend_first(3)
-    attend_last(3)
-    p_up(2)
-    att_wait(3)
-    p_up(6)
-    p_up(7)
-    p_down(5)
-    p_mine(3)
-    p_up(4)
-    p_mine(0)
-    p_down(7)
-    p_mine(1)
-    finish(3)
-    p_mine(4)
-    p_mine(6)
-    p_down(6)
-    p_mine(2)
-    p_down(4)
+    settle(10)
     finish(2)
+    finish(1)
     p_mine(7)
+    p_mine(5)
+    finish(4)
+    finish(5)
+    finish(6)
     finish(7)
     finish(0)
-    p_mine(5)
-    finish(1)
-    finish(6)
-    finish(5)
-    finish(4)
-    for copy, where in sent:
-        if where is None:
-            copy.wait_send()
-        else:
-            pl.when(where)(copy.wait_send)
+    settle(0)
 
 
 def shards(queries, keys, values, pairs, positions, w_out):

time: 101 us -> 101 us (level)
  no operation moved by 1% of the time
where the time goes in v4:
time: 101 us; the launch traced here: 100 us
  Pallas kernels  98.1 us (97%)
  local copies, waits for them, and re-layouts  2.29 us (2%)
    pallas_call x1, Pallas kernels, shards(): pl.pallas_call(kernel, out_shape=jax.ShapeDtypeStruct((BLK, 4096), bf16),...  98.1 us
    unnamed x1, local copies, waits for them, and re-layouts  2.29 us

profile of v4, /device:TPU:1, one launch (start us, length us, event | category | flops | bytes accessed | tf_op | source)
XLA Modules:
  0.0 100.4 jit_solution(16463801487397175217)
XLA Ops:
  0.0 98.1 %butterfly.1 = bf16[128,4096]{1,0:T(8,128)(2,1)} custom-call(bf16[1024,512]{1,0:T(8,128)(2,1)} %q_hbm.1, bf16[4,256,128]{2,1,0:T(8,128)(2,1)} %bitcast.3, bf16[4,256,128]{2,1,0:T(8,128)(2,1)} %bitcast.4, s32[8,8]{1,0:T(8,128)} %pairs_ref.1, s32[8,128]{1,0:T(8,128)} %bitcast.5, bf16[512,128]{1,0:T(8,128)(2,1)} %w_hbm.1), custom_call_target="tpu_custom_call" | custom-call | tf_op jit(solution)/shard_map/butterfly/pallas_call | solution.py:473
  98.1 2.3 %copy.8 = bf16[128,4096]{1,0:T(8,128)(2,1)} copy(bf16[128,4096]{1,0:T(8,128)(2,1)} %butterfly.1) | data formatting | bytes 2097152

commit v5 on v4

--- a/solution.py
+++ b/solution.py
@@ -324,145 +324,145 @@
     def attend_last(s):
         attend(chunk(s), core)
 
-    loads[0].wait()
-    z_forth(0)
     loads[1].wait()
     loads[2].wait()
     kv_own_y(1)
+    loads[0].wait()
+    z_forth(0)
+    pick()
+    spread(0)
     z_back(0)
-    pick()
+    kv_own_y(0)
     g_send()
-    spread(0)
+    kv_relay_y(1)
     z_forth(1)
     z_back(1)
     spread(2)
+    y_high(0)
+    kv_own_z(0)
     spread(1)
+    z_forth(2)
+    g_wait()
+    g_y_send()
+    z_back(2)
+    kv_own_y(2)
+    kv_relay_z(0)
+    spread(3)
+    kv_relay_y(0)
     y_low(0)
-    kv_own_y(0)
     kv_own_z(1)
-    kv_relay_y(1)
-    z_forth(2)
-    spread(3)
-    g_wait()
+    kv_relay_z(1)
     y_high(1)
-    z_back(2)
-    kv_own_z(0)
-    spread(4)
-    kv_relay_z(1)
-    g_y_send()
-    y_high(3)
-    y_high(0)
+    y_high(2)
+    z_forth(3)
     kv_own_z(2)
-    z_forth(3)
-    kv_own_y(2)
-    kv_relay_y(0)
-    kv_relay_z(0)
-    kv_relay2(0)
-    kv_relay2(1)
+    kv_wait_y(1)
     z_back(3)
     spread(5)
-    y_low(3)
+    spread(4)
+    y_high(3)
+    kv_relay2(0)
     y_low(1)
-    y_high(4)
+    kv_relay2(1)
+    far_step(0)
     kv_relay_z(2)
     z_forth(4)
-    y_high(5)
+    kv_wait_y(0)
+    spread(6)
+    g_y_wait()
     kv_relay_y(2)
-    far_step(3)
-    kv_own_z(3)
-    y_low(2)
-    g_y_wait()
-    kv_wait_y(0)
+    y_low(3)
+    kv_own_y(3)
     kv_wait_z(0)
     far_step(1)
-    spread(6)
-    far_step(0)
-    kv_relay2(2)
+    y_low(2)
     loads[3].wait()
     attend_first(0)
-    kv_own_y(3)
+    kv_relay2(2)
+    y_high(5)
+    w_wait(0)
+    kv_wait_z(1)
+    attend_last(0)
+    far_step(3)
+    attend_first(1)
+    att_wait(0)
+    spread(7)
+    y_low(5)
+    kv_own_z(3)
+    attend_last(1)
+    p_far(0)
     w_wait(3)
-    y_low(5)
-    y_high(2)
-    spread(7)
-    attend_last(0)
-    kv_wait_y(1)
-    kv_wait_z(1)
+    kv_wait_y(2)
+    y_low(4)
+    kv_wait_z(2)
+    far_step(5)
     w_wait(1)
-    attend_first(1)
-    w_wait(0)
-    far_step(5)
-    att_wait(0)
-    p_far(0)
+    p_far(1)
+    att_wait(1)
     p_far(3)
-    attend_last(1)
-    att_wait(1)
-    kv_relay_z(3)
-    kv_wait_y(2)
-    kv_wait_z(2)
-    p_far(1)
     far_step(2)
-    y_low(4)
-    p_up(1)
-    y_high(6)
+    p_up(3)
+    y_low(6)
     attend_first(2)
-    p_up(0)
+    w_wait(5)
+    y_high(4)
     y_high(7)
-    w_wait(2)
-    w_wait(5)
-    y_low(6)
     y_low(7)
     p_far(5)
+    p_up(0)
+    far_step(4)
+    attend_last(2)
+    kv_relay_z(3)
+    att_wait(2)
+    y_high(6)
+    p_up(1)
+    w_wait(4)
+    far_step(7)
+    p_down(0)
+    w_wait(2)
+    p_down(1)
+    p_down(4)
+    kv_relay_y(3)
     p_far(2)
-    attend_last(2)
-    kv_relay_y(3)
-    far_step(4)
-    att_wait(2)
+    kv_relay2(3)
+    far_step(6)
     p_down(3)
-    p_down(2)
-    p_up(3)
-    kv_relay2(3)
-    w_wait(4)
-    far_step(6)
+    w_wait(7)
     p_far(4)
+    p_up(2)
+    kv_wait_y(3)
     p_down(5)
-    far_step(7)
-    p_up(2)
-    w_wait(7)
-    kv_wait_y(3)
     w_wait(6)
-    p_down(4)
     kv_wait_z(3)
+    p_far(6)
     attend_first(3)
     p_far(7)
-    p_far(6)
+    p_up(4)
+    attend_last(3)
+    p_down(2)
+    att_wait(3)
+    p_mine(1)
+    p_mine(0)
+    p_mine(5)
+    p_up(6)
     p_down(6)
-    p_up(4)
-    att_wait(3)
-    attend_last(3)
-    p_down(1)
+    p_up(5)
+    p_mine(4)
+    finish(0)
+    p_mine(2)
+    p_mine(7)
+    p_down(7)
+    finish(1)
     p_up(7)
-    p_up(5)
-    p_mine(2)
-    p_mine(3)
-    finish(3)
-    p_mine(0)
-    p_mine(1)
+    settle(10)
     p_mine(6)
-    p_up(6)
-    p_mine(4)
-    p_down(7)
-    p_down(0)
-    settle(10)
-    finish(2)
-    finish(1)
-    p_mine(7)
-    p_mine(5)
-    finish(4)
     finish(5)
     finish(6)
+    p_mine(3)
+    finish(4)
+    finish(3)
+    finish(2)
     finish(7)
-    finish(0)
     settle(0)
 
 

time: 101 us -> 101 us (level); the launches traced: 100 us -> 99.2 us
  Pallas kernels: 98.1 us -> 96.9 us
    pallas_call x1, Pallas kernels: 98.1 us -> 96.9 us  [shards(): pl.pallas_call(kernel, out_shape=jax.ShapeDtypeStruct((BLK, 4096), bf16),...]
where the time goes in v5:
time: 101 us; the launch traced here: 99.2 us
  Pallas kernels  96.9 us (96%)
  local copies, waits for them, and re-layouts  2.29 us (2%)
    pallas_call x1, Pallas kernels, shards(): pl.pallas_call(kernel, out_shape=jax.ShapeDtypeStruct((BLK, 4096), bf16),...  96.9 us
    unnamed x1, local copies, waits for them, and re-layouts  2.29 us

profile of v5, /device:TPU:1, one launch (start us, length us, event | category | flops | bytes accessed | tf_op | source)
XLA Modules:
  0.0 99.2 jit_solution(1932077542613478958)
XLA Ops:
  0.0 96.9 %butterfly.1 = bf16[128,4096]{1,0:T(8,128)(2,1)} custom-call(bf16[1024,512]{1,0:T(8,128)(2,1)} %q_hbm.1, bf16[4,256,128]{2,1,0:T(8,128)(2,1)} %bitcast.3, bf16[4,256,128]{2,1,0:T(8,128)(2,1)} %bitcast.4, s32[8,8]{1,0:T(8,128)} %pairs_ref.1, s32[8,128]{1,0:T(8,128)} %bitcast.5, bf16[512,128]{1,0:T(8,128)(2,1)} %w_hbm.1), custom_call_target="tpu_custom_call" | custom-call | tf_op jit(solution)/shard_map/butterfly/pallas_call | solution.py:473
  96.9 2.3 %copy.8 = bf16[128,4096]{1,0:T(8,128)(2,1)} copy(bf16[128,4096]{1,0:T(8,128)(2,1)} %butterfly.1) | data formatting | bytes 2097152
